TPU v7x, 256 devices: a whole 4x4x8 slice. The times are simulated.
256 devices in a mesh: seq: 32 (over z, x), exp: 8 (over y, core).
Axes of the slice: x: 4, y: 4, z: 8, core: 2. Of those that a mesh axis runs over, the one named last changes fastest.
Arguments:
- mixer_input: bfloat16 [2048, 8192], P('seq', 'exp'), may hold values from -6 to 6
- gate_input: bfloat16 [2048, 8192], P('seq', 'exp'), may hold values from -6 to 6
- conv_weight: bfloat16 [4, 8192], P(None, 'exp'), may hold values from -3 to 3
- conv_bias: float32 [8192], P('exp'), may hold values from -3 to 3
- rank_weight: bfloat16 [8192, 256], P('exp'), may hold values from -0.0625 to 0.0625
- state_weight: bfloat16 [8192, 32], P('exp'), may hold values from -0.03125 to 0.03125
- delta_weight: bfloat16 [256, 8192], P(None, 'exp'), may hold values from -0.375 to 0.375
- delta_bias: float32 [8192], P('exp'), may hold values from -1 to 1
- log_rates: float32 [16, 8192], P(None, 'exp'), may hold values from -10 to -1
- skip_gain: float32 [8192], P('exp'), may hold values from 0.5 to 1.5
- out_proj: bfloat16 [8192, 4096], P('exp', 'seq'), may hold values from -0.0625 to 0.0625
- residual: bfloat16 [2048, 4096], P(('seq', 'exp')), may hold values from -3 to 3
- norm_gain: float32 [4096], replicated, may hold values from 0.5 to 1.5
- router: float32 [4096, 8], replicated, may hold values from -0.09375 to 0.09375
- w_gate: bfloat16 [8, 4096, 14336], P('exp', None, 'seq'), may hold values from -0.09375 to 0.09375
- w_up: bfloat16 [8, 4096, 14336], P('exp', None, 'seq'), may hold values from -0.09375 to 0.09375
- w_down: bfloat16 [8, 14336, 4096], P('exp', 'seq'), may hold values from -0.09375 to 0.09375
- routes: int32 [2048, 2], P(('seq', 'exp')), may hold values from 0 to 7, all different within a row; in each aligned block of 8 rows (0 to 7, 8 to 15, ...) at most 4 rows name the same one
Outputs:
- layer_out: bfloat16 [2048, 4096], P(('seq', 'exp'))
- expert_mix: float32 [2048, 4096], P(('seq', 'exp'))
Inputs may be any that keep to these rules, and one draw needn't show every extreme that they name: `routes`: each row names two different experts; among the 8 rows of one device no expert is named more than 4 times, a bound that some block reaches there on some device.
All inputs are finite; a program needn't handle non-finite values.
Results may differ from a plain program's by a relative error of at most 0.024.
Values may be sent and summed in bfloat16 or wider, within the bound.
No kernel may reach another device: no remote copies, remote signals or barrier semaphores. Data moves between devices by JAX's collectives and lax.ppermute only.
A program may use at most 128 MiB of HBM per device.

v0:
```python
import jax
import jax.numpy as jnp
from jax import lax
from jax.sharding import PartitionSpec as P


def shifted(block, axis, distance):
    devices = range(lax.axis_size(axis))
    route = [(i - distance, i) for i in devices if i - distance in devices]
    return lax.ppermute(block, axis, route)


def entering(array, axis, combine, identity):
    count, index = (lax.axis_size(axis), lax.axis_index(axis))
    everything = jax.tree.map(lambda part: lax.all_gather(part, axis), array)
    start = jax.tree.map(
        lambda part, zero: jnp.broadcast_to(jnp.asarray(zero, part.dtype), part.shape),
        array,
        identity,
    )

    def hop(k, before):
        reached = k < index
        new = combine(before, jax.tree.map(lambda part: part[k], everything))
        return jax.tree.map(lambda a, b: jnp.where(reached, a, b), new, before)

    return lax.fori_loop(0, count, hop, start)


def combine_pair(earlier, following):
    return (earlier[0] * following[0], following[0] * earlier[1] + following[1])


def body(
    mixer_input,
    gate_input,
    conv_weight,
    conv_bias,
    rank_weight,
    state_weight,
    delta_weight,
    delta_bias,
    log_rates,
    skip_gain,
    out_proj,
    residual,
    norm_gain,
    router,
    w_gate,
    w_up,
    w_down,
    routes,
):
    taps = conv_weight.shape[0]
    block_rows = mixer_input.shape[0]
    rim_rows = shifted(mixer_input[block_rows - (taps - 1) :], "seq", 1)
    padded = jnp.concatenate([rim_rows, mixer_input], axis=0)
    conv_sum = jnp.zeros(mixer_input.shape, jnp.float32) + conv_bias[None, :]
    for offset in range(taps):
        conv_sum = conv_sum + conv_weight[offset].astype(jnp.float32)[None, :] * padded[
            offset : offset + block_rows
        ].astype(jnp.float32)
    conv_act = jax.nn.silu(conv_sum).astype(jnp.bfloat16)
    delta_part = jnp.dot(conv_act, rank_weight, preferred_element_type=jnp.float32)
    state_part = jnp.dot(conv_act, state_weight, preferred_element_type=jnp.float32)
    delta_sum, state_maps = lax.psum((delta_part, state_part), "exp")
    delta_low = delta_sum.astype(jnp.bfloat16)
    states = log_rates.shape[0]
    input_map = state_maps[:, :states]
    output_map = state_maps[:, states:]
    delta = jax.nn.softplus(
        jnp.dot(delta_low, delta_weight, preferred_element_type=jnp.float32) + delta_bias[None, :]
    )
    decay_rate = jnp.exp(log_rates)
    conv_float = conv_act.astype(jnp.float32)
    driven = (delta * conv_float)[:, None, :] * input_map[:, :, None]
    decays = jnp.exp(-delta[:, None, :] * decay_rate[None])
    passed = jnp.cumsum(delta, axis=0)
    total_dt = passed[-1]
    weights_left = jnp.exp(-(total_dt[None, :] - passed)[:, None, :] * decay_rate[None])
    transform = (jnp.exp(-total_dt[None, :] * decay_rate), jnp.sum(weights_left * driven, axis=0))
    incoming = entering(
        transform, "seq", combine_pair, (jnp.ones_like(decay_rate), jnp.zeros_like(decay_rate))
    )
    start_state = incoming[1]

    def advance(carried, inputs):
        decay_t, driven_t, output_t = inputs
        carried = decay_t * carried + driven_t
        return (carried, jnp.sum(output_t[:, None] * carried, axis=0))

    last_state, scan_out = lax.scan(advance, start_state, (decays, driven, output_map))
    scan_out = scan_out + skip_gain[None, :] * conv_float
    gated = (scan_out * jax.nn.silu(gate_input.astype(jnp.float32))).astype(jnp.bfloat16)
    tok_dev = residual.shape[0]
    partial_value = jnp.dot(
        gated,
        lax.all_gather(out_proj, "seq", axis=1, tiled=True),
        preferred_element_type=jnp.float32,
    )
    mamba_out = lax.psum_scatter(partial_value, "exp", scatter_dimension=0, tiled=True)
    hidden = residual.astype(jnp.float32) + mamba_out
    mean_square = jnp.mean(hidden * hidden, axis=1, keepdims=True)
    normed = (hidden * lax.rsqrt(mean_square + 1e-05) * norm_gain[None, :]).astype(jnp.bfloat16)
    logits = jnp.dot(normed.astype(jnp.float32), router, precision=lax.Precision.HIGHEST)
    experts = router.shape[1]
    expert_ids = jnp.arange(experts, dtype=jnp.int32)
    matches = (routes[:, :, None] == expert_ids[None, None, :]).astype(jnp.float32)
    chosen = jnp.sum(matches * logits[:, None, :], axis=2)
    route_weights = jax.nn.sigmoid(chosen - chosen[:, ::-1])
    capacity = max(2, 4 * tok_dev // experts)
    flat_ids = routes.reshape(-1)
    route_pos = jnp.arange(flat_ids.shape[0], dtype=jnp.int32)
    earlier_same = (flat_ids[:, None] == flat_ids[None, :]) & (
        route_pos[None, :] < route_pos[:, None]
    )
    slot_rank = jnp.sum(earlier_same.astype(jnp.int32), axis=1)
    slot_of = flat_ids * capacity + slot_rank
    slot_ids = jnp.arange(experts * capacity, dtype=jnp.int32)
    placing = (slot_ids[:, None] == slot_of[None, :]).astype(jnp.bfloat16)
    repeated = jnp.repeat(normed, 2, axis=0)
    outbound = jnp.dot(placing, repeated, preferred_element_type=jnp.float32).astype(jnp.bfloat16)
    arrived = lax.all_to_all(outbound, "exp", split_axis=0, concat_axis=0, tiled=True)
    gate_local = w_gate[0]
    up_local = w_up[0]
    down_local = w_down[0]
    shard_part = lax.all_gather(arrived, "seq", axis=0, tiled=True)
    gate_part = jnp.dot(shard_part, gate_local, preferred_element_type=jnp.float32)
    up_part = jnp.dot(shard_part, up_local, preferred_element_type=jnp.float32)
    activated = (jax.nn.silu(gate_part) * up_part).astype(jnp.bfloat16)
    expert_out = lax.psum_scatter(
        jnp.dot(activated, down_local, preferred_element_type=jnp.float32).astype(jnp.bfloat16),
        "seq",
        scatter_dimension=0,
        tiled=True,
    ).astype(jnp.float32)
    returned = lax.all_to_all(expert_out, "exp", split_axis=0, concat_axis=0, tiled=True)
    picked = jnp.take(returned, slot_of, axis=0)
    moe_sum = jnp.sum(picked.reshape(tok_dev, 2, -1) * route_weights[:, :, None], axis=1)
    return ((hidden + moe_sum).astype(jnp.bfloat16), moe_sum)


def solution(mesh):
    in_specs = (
        P("seq", "exp"),
        P("seq", "exp"),
        P(None, "exp"),
        P("exp"),
        P("exp", None),
        P("exp", None),
        P(None, "exp"),
        P("exp"),
        P(None, "exp"),
        P("exp"),
        P("exp", "seq"),
        P(("seq", "exp"), None),
        P(),
        P(),
        P("exp", None, "seq"),
        P("exp", None, "seq"),
        P("exp", "seq", None),
        P(("seq", "exp"), None),
    )
    out_specs = (P(("seq", "exp"), None), P(("seq", "exp"), None))
    return jax.shard_map(body, mesh=mesh, in_specs=in_specs, out_specs=out_specs, check_vma=False)
```

profile of v0, /device:TPU:1, one launch (start us, length us, event | category | flops | bytes accessed | tf_op | source)
XLA Modules:
  0.0 738.1 jit_solution(16103797339628601987)
XLA Ops:
  8.0 3.9 collective-permute-start
  12.8 1.4 multiply_convert_fusion.1
  14.2 1.2 fusion.34
  15.4 1.0 fusion.35
  16.4 23.9 %all-reduce = (bf16[64,256]{1,0:T(8,128)(2,1)S(1)}, f32[64,32]{0,1:T(8,128)S(1)}) all-reduce(f32[64,256]{1,0:T(8,128)S(1)} %fusion.34, f32[64,32]{0,1:T(8,128)S(1)} %fusion.35), channel_id=1, replica_groups=mesh['seq'=32,'exp'=8] {'exp'}, use_global_device_ids=true, to_apply=%region_0.1 | all-reduce | flops 18432 | bytes 114688 | tf_op jit(solution)/shard_map/psum | solution.py:66
  40.3 1.0 fusion.30
  41.7 1.5 fusion.32
  43.2 4.3 broadcast_multiply_fusion
  49.2 77.0 %all-gather.13.cloned.1.call-done = f32[512,1024]{1,0:T(8,128)} async-done(((f32[16,1024]{1,0:T(8,128)}), f32[512,1024]{1,0:T(8,128)}) %all-gather.13.cloned.1.call-update) | async-done | bytes 2097168 | tf_op jit(solution)/shard_map/all_gather | solution.py:15
  126.2 78.3 %all-gather.11.cloned.1.call-done = f32[512,1024]{1,0:T(8,128)} async-done(((f32[16,1024]{1,0:T(8,128)}), f32[512,1024]{1,0:T(8,128)}) %all-gather.11.cloned.1.call-update) | async-done | bytes 2097168 | tf_op jit(solution)/shard_map/all_gather | solution.py:15
  204.5 30.0 %while.29 = (s32[]{:T(128)}, f32[16,1024]{1,0:T(8,128)S(1)}, s32[]{:T(128)}, f32[32,16,1024]{2,1,0:T(8,128)}, f32[32,16,1024]{2,1,0:T(8,128)}) while((s32[]{:T(128)}, f32[16,1024]{1,0:T(8,128)S(1)}, s32[]{:T(128)}, f32[32,16,1024]{2,1,0:T(8,128)}, f32[32,16,1024]{2,1,0:T(8,128)}) %tuple.91), condition=%wide.region_5.6_spmd.clone.clone, body=%wide.region_4.5_spmd.clone.sunk.clone | while | flops 65540 | bytes 262229 | solution.py:27
  234.5 71.4 %while.28 = (s32[]{:T(128)}, f32[16,1024]{1,0:T(8,128)S(1)}, f32[64,1024]{1,0:T(8,128)S(1)}, f32[64,16,1024]{2,1,0:T(8,128)}, f32[64,16,1024]{2,1,0:T(8,128)}, /*index=5*/f32[64,16]{1,0:T(8,128)S(1)}) while((s32[]{:T(128)}, f32[16,1024]{1,0:T(8,128)S(1)}, f32[64,1024]{1,0:T(8,128)S(1)}, f32[64,16,1024]{2,1,0:T(8,128)}, ...), condition=%wide.region_8.9_spmd.clone, body=%wide.region_6.8_spmd.sunk.clone | while | flops 64514 | bytes 274705 | solution.py:92
  234.5 1.0 multiply_reduce_fusion.6
  236.8 1.0 multiply_reduce_fusion.6
  237.9 1.0 multiply_reduce_fusion.6
  239.0 1.0 multiply_reduce_fusion.6
  240.1 1.0 multiply_reduce_fusion.6
  241.2 1.0 multiply_reduce_fusion.6
  242.4 1.0 multiply_reduce_fusion.6
  243.5 1.0 multiply_reduce_fusion.6
  244.6 1.0 multiply_reduce_fusion.6
  245.7 1.0 multiply_reduce_fusion.6
  246.8 1.0 multiply_reduce_fusion.6
  247.9 1.0 multiply_reduce_fusion.6
  249.0 1.0 multiply_reduce_fusion.6
  250.2 1.0 multiply_reduce_fusion.6
  260.2 1.0 multiply_reduce_fusion.6
  261.3 1.0 multiply_reduce_fusion.6
  262.4 1.0 multiply_reduce_fusion.6
  263.5 1.0 multiply_reduce_fusion.6
  264.7 1.0 multiply_reduce_fusion.6
  270.2 1.0 multiply_reduce_fusion.6
  271.4 1.0 multiply_reduce_fusion.6
  274.7 1.0 multiply_reduce_fusion.6
  275.8 1.0 multiply_reduce_fusion.6
  276.9 1.0 multiply_reduce_fusion.6
  278.1 1.0 multiply_reduce_fusion.6
  279.2 1.0 multiply_reduce_fusion.6
  284.8 1.0 multiply_reduce_fusion.6
  285.9 1.0 multiply_reduce_fusion.6
  287.0 1.0 multiply_reduce_fusion.6
  288.1 1.0 multiply_reduce_fusion.6
  289.2 1.0 multiply_reduce_fusion.6
  290.4 1.0 multiply_reduce_fusion.6
  291.5 1.0 multiply_reduce_fusion.6
  292.6 1.0 multiply_reduce_fusion.6
  293.7 1.0 multiply_reduce_fusion.6
  298.2 1.0 multiply_reduce_fusion.6
  299.3 1.0 multiply_reduce_fusion.6
  300.4 1.0 multiply_reduce_fusion.6
  304.9 1.0 multiply_reduce_fusion.6
  306.0 3.2 all-gather.7.cloned.1.call-done
  309.2 6.1 fusion.20
  315.7 32.0 %reduce-scatter.3.cloned.1.call-done = f32[8,4096]{1,0:T(8,128)} async-done(((f32[64,4096]{1,0:T(8,128)}), f32[8,4096]{1,0:T(8,128)}) %reduce-scatter.3.cloned.1.call-update) | async-done | bytes 131088 | tf_op jit(solution)/shard_map/reduce_scatter | solution.py:101
  347.7 1.1 multiply_reduce_fusion.3
  348.8 1.0 multiply_convert_fusion.2
  350.2 12.0 %all_to_all.28 = bf16[8,4,4096]{2,1,0:T(4,128)(2,1)S(1)} all-to-all(bf16[8,4,4096]{2,1,0:T(4,128)(2,1)S(1)} %all_to_all.18), channel_id=1, replica_groups=mesh['seq'=32,'exp'=8] {'exp'}, dimensions={0} | all-to-all | bytes 524288 | tf_op jit(solution)/shard_map/all_to_all | solution.py:123
  363.3 97.7 %all-gather.9.cloned.1.call-done = bf16[1024,4096]{1,0:T(8,128)(2,1)} async-done(((bf16[32,4096]{1,0:T(8,128)(2,1)}), bf16[1024,4096]{1,0:T(8,128)(2,1)}) %all-gather.9.cloned.1.call-update) | async-done | bytes 8388624 | tf_op jit(solution)/shard_map/all_gather | solution.py:127
  460.9 9.7 %fusion.5 = f32[1024,448]{0,1:T(8,128)} fusion(bf16[1024,4096]{1,0:T(8,128)(2,1)} %all-gather.9.cloned.1.call-done, bf16[1,4096,448]{1,2,0:T(8,128)(2,1)} %param.36), kind=kOutput, calls=%fused_computation.16 | convolution fusion | flops 3758096384 | bytes 13893632 | tf_op jit(solution)/shard_map/dot_general | solution.py:128
  470.6 15.4 %convolution_convert_fusion = bf16[1024,4096]{1,0:T(8,128)(2,1)} fusion(bf16[1,448,4096]{2,1,0:T(8,128)(2,1)} %param.38, f32[1024,448]{0,1:T(8,128)} %fusion.5, bf16[1024,4096]{1,0:T(8,128)(2,1)} %all-gather.9.cloned.1.call-done, bf16[1,4096,448]{1,2,0:T(8,128)(2,1)} %param.37), kind=kOutput, calls=%fused_computation.9 | convolution fusion | flops 7523139584 | bytes 25952256 | tf_op jit(solution)/shard_map/dot_general | solution.py:132
  486.3 222.6 %reduce-scatter.5.cloned.1.call-done = bf16[32,4096]{1,0:T(8,128)(2,1)} async-done(((bf16[1024,4096]{1,0:T(8,128)(2,1)}), bf16[32,4096]{1,0:T(8,128)(2,1)}) %reduce-scatter.5.cloned.1.call-update) | async-done | bytes 262160 | tf_op jit(solution)/shard_map/reduce_scatter | solution.py:131
  708.9 1.9 reshape.112
  710.8 8.9 %all-to-all-start.1 = ((f32[8,4,4096]{2,1,0:T(4,128)}), f32[8,4,4096]{2,1,0:T(4,128)S(1)}, u32[]{:S(2)}, u32[]{:S(2)}) async-start(f32[8,4,4096]{2,1,0:T(4,128)} %reshape.112), calls=%async_computation.3 | async-start | bytes 1048576 | tf_op jit(solution)/shard_map/all_to_all | solution.py:137
  720.2 9.0 %all-to-all-done.1 = f32[8,4,4096]{2,1,0:T(4,128)S(1)} async-done(((f32[8,4,4096]{2,1,0:T(4,128)}), f32[8,4,4096]{2,1,0:T(4,128)S(1)}, u32[]{:S(2)}, u32[]{:S(2)}) %all-to-all-start.1) | async-done | bytes 524320 | tf_op jit(solution)/shard_map/all_to_all | solution.py:137
  (252 shorter events, 69.4 us)
Async XLA Ops:
  7.2 33.1 %copy-start = (bf16[256,1024]{1,0:T(8,128)(2,1)S(1)}, bf16[256,1024]{1,0:T(8,128)(2,1)}, u32[]{:S(2)}) copy-start(bf16[256,1024]{1,0:T(8,128)(2,1)} %param.28) | copy-start | bytes 1572868
  7.2 119.0 %all-gather.13.cloned.1.call-start = ((), (), s32[]{:S(2)}) async-start(), calls=%async_computation.9 | async-start | bytes 2162688 | tf_op jit(solution)/shard_map/all_gather | solution.py:15
  8.0 4.8 collective-permute-start
  43.2 265.9 %copy-start.4 = (bf16[64,1024]{1,0:T(8,128)(2,1)S(1)}, bf16[64,1024]{1,0:T(8,128)(2,1)}, u32[]{:S(2)}) copy-start(bf16[64,1024]{1,0:T(8,128)(2,1)} %param.23) | copy-start | bytes 393220
  43.2 265.9 %copy-start.6 = (f32[1024]{0:T(1024)S(1)}, f32[1024]{0:T(1024)}, u32[]{:S(2)}) copy-start(f32[1024]{0:T(1024)} %param.31) | copy-start | bytes 12292
  47.6 157.0 %all-gather.11.cloned.1.call-start = ((), (), s32[]{:S(2)}) async-start(), calls=%async_computation.8 | async-start | bytes 2162688 | tf_op jit(solution)/shard_map/all_gather | solution.py:15
  48.3 260.9 %all-gather.7.cloned.1.call-start = ((), (), s32[]{:S(2)}) async-start(), calls=%async_computation.4 | async-start | bytes 8650752 | tf_op jit(solution)/shard_map/all_gather | solution.py:98
  49.0 298.7 %reduce-scatter.3.cloned.1.call-start = ((), (), s32[]{:S(2)}) async-start(), calls=%async_computation.5 | async-start | bytes 1179648 | tf_op jit(solution)/shard_map/reduce_scatter | solution.py:101
  309.2 6.2 copy-start.8
  309.2 38.5 %copy-start.2 = (bf16[8,4096]{1,0:T(8,128)(2,1)S(1)}, bf16[8,4096]{1,0:T(8,128)(2,1)}, u32[]{:S(2)}) copy-start(bf16[8,4096]{1,0:T(8,128)(2,1)} %param.33) | copy-start | bytes 196612
  309.2 39.6 %copy-start.7 = (f32[4096]{0:T(1024)S(1)}, f32[4096]{0:T(1024)}, u32[]{:S(2)}) copy-start(f32[4096]{0:T(1024)} %param.34) | copy-start | bytes 49156
  315.3 145.7 %all-gather.9.cloned.1.call-start = ((), (), s32[]{:S(2)}) async-start(), calls=%async_computation.6 | async-start | bytes 8650752 | tf_op jit(solution)/shard_map/all_gather | solution.py:127
  363.1 345.9 %reduce-scatter.5.cloned.1.call-start = ((), (), s32[]{:S(2)}) async-start(), calls=%async_computation.7 | async-start | bytes 8650752 | tf_op jit(solution)/shard_map/reduce_scatter | solution.py:131
  486.0 233.6 %copy-start.5 = (f32[4096,8]{0,1:T(8,128)S(1)}, f32[4096,8]{0,1:T(8,128)}, u32[]{:S(2)}) copy-start(f32[4096,8]{0,1:T(8,128)} %param.35) | copy-start | bytes 393220
  486.1 244.5 %copy-start.1 = (f32[8,4096]{1,0:T(8,128)S(1)}, f32[8,4096]{1,0:T(8,128)}, u32[]{:S(2)}) copy-start(f32[8,4096]{1,0:T(8,128)} %reduce-scatter.3.cloned.1.call-done) | copy-start | bytes 393220
  710.8 18.3 %all-to-all-start.1 = ((f32[8,4,4096]{2,1,0:T(4,128)}), f32[8,4,4096]{2,1,0:T(4,128)S(1)}, u32[]{:S(2)}, u32[]{:S(2)}) async-start(f32[8,4,4096]{2,1,0:T(4,128)} %reshape.112), calls=%async_computation.3 | async-start | bytes 1048576 | tf_op jit(solution)/shard_map/all_to_all | solution.py:137
  730.6 0.7 copy-start.3
Sparse Core Ops, SparseCore 0:
  47.7 78.5 all-gather.12
  129.4 75.1 all-gather.10
  207.0 102.1 all-gather.6
  315.4 32.2 reduce-scatter.2
  363.2 97.7 all-gather.8
  486.2 222.6 reduce-scatter.4
where the time goes:
time: 743 us; the launch traced here: 738 us
  waiting for transfers between devices  521 us (70%)
  other arithmetic  103 us (14%)
  blocking collectives  35.9 us (5%)
  matrix products  34.8 us (5%)
  between operations  14.4 us (2%)
  starting transfers between devices  13.2 us (2%)
  local copies, waits for them, and re-layouts  13 us (2%)
    reduce_scatter x1, waiting for transfers between devices, body(): lax.psum_scatter(jnp.dot(activated, down_local, preferred_element_type=jn...  223 us
    all_gather x2, waiting for transfers between devices, entering(): everything = jax.tree.map(lambda part: lax.all_gather(part, axis), array)  155 us
    all_gather x1, waiting for transfers between devices, body(): shard_part = lax.all_gather(arrived, 'seq', axis=0, tiled=True)  97.7 us
    reduce_sum x64, other arithmetic, advance(): return (carried, jnp.sum(output_t[:, None] * carried, axis=0))  61.7 us
    reduce_scatter x1, waiting for transfers between devices, body(): lax.psum_scatter(partial_value, 'exp', scatter_dimension=0, tiled=True)  32 us
    select_n x32, other arithmetic, hop(): return jax.tree.map(lambda a, b: jnp.where(reached, a, b), new, before)  29.3 us
    psum x1, blocking collectives, body(): delta_sum, state_maps = lax.psum((delta_part, state_part), 'exp')  23.9 us
    dot_general x1, matrix products, body(): jnp.dot(activated, down_local, preferred_element_type=jnp.float32)  15.4 us
  transfers between devices with their start and end apart: 8, of which 7 were waited for; matrix products, arithmetic and copies ran while one was open for 14% of the time, Pallas kernels for 0%

commit v1 on v0

--- a/solution.py
+++ b/solution.py
@@ -124,7 +124,9 @@
     gate_local = w_gate[0]
     up_local = w_up[0]
     down_local = w_down[0]
-    shard_part = lax.all_gather(arrived, "seq", axis=0, tiled=True)
+    shard_part = jnp.concatenate(
+        lax.all_to_all(jnp.stack([arrived] * lax.axis_size("seq")), "seq", 0, 0), axis=0
+    )
     gate_part = jnp.dot(shard_part, gate_local, preferred_element_type=jnp.float32)
     up_part = jnp.dot(shard_part, up_local, preferred_element_type=jnp.float32)
     activated = (jax.nn.silu(gate_part) * up_part).astype(jnp.bfloat16)

time: 743 us -> 837 us (1.13)
  blocking collectives: 35.9 us -> 229 us
  waiting for transfers between devices: 521 us -> 423 us
    all_to_all x0 -> x1, blocking collectives: none -> 193 us  [body(): lax.all_to_all(jnp.stack([arrived] * lax.axis_size('seq')), 'seq', 0, 0)]
    all_gather x1 -> x0, waiting for transfers between devices: 97.7 us -> none  [body(): shard_part = lax.all_gather(arrived, 'seq', axis=0, tiled=True)]
  transfers between devices with their start and end apart: 8 -> 7, of which waited for: 7 -> 6; matrix products, arithmetic and copies ran while one was open for 14% -> 12% of each run, Pallas kernels for 0% -> 0%
where the time goes in v1:
time: 837 us; the launch traced here: 832 us
  waiting for transfers between devices  423 us (51%)
  blocking collectives  229 us (27%)
  other arithmetic  103 us (12%)
  matrix products  30.4 us (4%)
  local copies, waits for them, and re-layouts  16.6 us (2%)
  between operations  14.1 us (2%)
  starting transfers between devices  13.1 us (2%)
    reduce_scatter x1, waiting for transfers between devices, body(): lax.psum_scatter(jnp.dot(activated, down_local, preferred_element_type=jn...  223 us
    all_to_all x1, blocking collectives, body(): lax.all_to_all(jnp.stack([arrived] * lax.axis_size('seq')), 'seq', 0, 0)  193 us
    all_gather x2, waiting for transfers between devices, entering(): everything = jax.tree.map(lambda part: lax.all_gather(part, axis), array)  155 us
    reduce_sum x64, other arithmetic, advance(): return (carried, jnp.sum(output_t[:, None] * carried, axis=0))  61.7 us
    reduce_scatter x1, waiting for transfers between devices, body(): lax.psum_scatter(partial_value, 'exp', scatter_dimension=0, tiled=True)  31.9 us
    select_n x32, other arithmetic, hop(): return jax.tree.map(lambda a, b: jnp.where(reached, a, b), new, before)  29.3 us
    psum x1, blocking collectives, body(): delta_sum, state_maps = lax.psum((delta_part, state_part), 'exp')  23.9 us
  transfers between devices with their start and end apart: 7, of which 6 were waited for; matrix products, arithmetic and copies ran while one was open for 12% of the time, Pallas kernels for 0%

profile of v1, /device:TPU:1, one launch (start us, length us, event | category | flops | bytes accessed | tf_op | source)
XLA Modules:
  0.0 831.9 jit_solution(14557272979420904484)
XLA Ops:
  8.0 3.9 collective-permute-start
  12.8 1.4 multiply_convert_fusion.1
  14.2 1.2 fusion.34
  15.4 1.0 fusion.35
  16.4 23.9 %all-reduce = (bf16[64,256]{1,0:T(8,128)(2,1)S(1)}, f32[64,32]{0,1:T(8,128)S(1)}) all-reduce(f32[64,256]{1,0:T(8,128)S(1)} %fusion.34, f32[64,32]{0,1:T(8,128)S(1)} %fusion.35), channel_id=1, replica_groups=mesh['seq'=32,'exp'=8] {'exp'}, use_global_device_ids=true, to_apply=%region_0.1 | all-reduce | flops 18432 | bytes 114688 | tf_op jit(solution)/shard_map/psum | solution.py:66
  40.3 1.0 fusion.30
  41.7 1.5 fusion.32
  43.2 4.3 broadcast_multiply_fusion
  49.2 77.0 %all-gather.10.cloned.1.call-done = f32[512,1024]{1,0:T(8,128)} async-done(((f32[16,1024]{1,0:T(8,128)}), f32[512,1024]{1,0:T(8,128)}) %all-gather.10.cloned.1.call-update) | async-done | bytes 2097168 | tf_op jit(solution)/shard_map/all_gather | solution.py:15
  126.2 78.3 %all-gather.8.cloned.1.call-done = f32[512,1024]{1,0:T(8,128)} async-done(((f32[16,1024]{1,0:T(8,128)}), f32[512,1024]{1,0:T(8,128)}) %all-gather.8.cloned.1.call-update) | async-done | bytes 2097168 | tf_op jit(solution)/shard_map/all_gather | solution.py:15
  204.5 30.0 %while.29 = (s32[]{:T(128)}, f32[16,1024]{1,0:T(8,128)S(1)}, s32[]{:T(128)}, f32[32,16,1024]{2,1,0:T(8,128)}, f32[32,16,1024]{2,1,0:T(8,128)}) while((s32[]{:T(128)}, f32[16,1024]{1,0:T(8,128)S(1)}, s32[]{:T(128)}, f32[32,16,1024]{2,1,0:T(8,128)}, f32[32,16,1024]{2,1,0:T(8,128)}) %tuple.89), condition=%wide.region_5.6_spmd.clone.clone, body=%wide.region_4.5_spmd.clone.sunk.clone | while | flops 65540 | bytes 262229 | solution.py:27
  234.5 71.4 %while.28 = (s32[]{:T(128)}, f32[16,1024]{1,0:T(8,128)S(1)}, f32[64,1024]{1,0:T(8,128)S(1)}, f32[64,16,1024]{2,1,0:T(8,128)}, f32[64,16,1024]{2,1,0:T(8,128)}, /*index=5*/f32[64,16]{1,0:T(8,128)S(1)}) while((s32[]{:T(128)}, f32[16,1024]{1,0:T(8,128)S(1)}, f32[64,1024]{1,0:T(8,128)S(1)}, f32[64,16,1024]{2,1,0:T(8,128)}, ...), condition=%wide.region_8.9_spmd.clone, body=%wide.region_6.8_spmd.sunk.clone | while | flops 64514 | bytes 274705 | solution.py:92
  234.5 1.0 multiply_reduce_fusion.6
  235.7 1.0 multiply_reduce_fusion.6
  236.8 1.0 multiply_reduce_fusion.6
  237.9 1.0 multiply_reduce_fusion.6
  239.0 1.0 multiply_reduce_fusion.6
  240.1 1.0 multiply_reduce_fusion.6
  241.2 1.0 multiply_reduce_fusion.6
  242.4 1.0 multiply_reduce_fusion.6
  243.5 1.0 multiply_reduce_fusion.6
  244.6 1.0 multiply_reduce_fusion.6
  245.7 1.0 multiply_reduce_fusion.6
  246.8 1.0 multiply_reduce_fusion.6
  260.2 1.0 multiply_reduce_fusion.6
  261.3 1.0 multiply_reduce_fusion.6
  262.4 1.0 multiply_reduce_fusion.6
  263.6 1.0 multiply_reduce_fusion.6
  264.7 1.0 multiply_reduce_fusion.6
  270.2 1.0 multiply_reduce_fusion.6
  271.4 1.0 multiply_reduce_fusion.6
  274.7 1.0 multiply_reduce_fusion.6
  275.8 1.0 multiply_reduce_fusion.6
  276.9 1.0 multiply_reduce_fusion.6
  278.1 1.0 multiply_reduce_fusion.6
  279.2 1.0 multiply_reduce_fusion.6
  284.8 1.0 multiply_reduce_fusion.6
  285.9 1.0 multiply_reduce_fusion.6
  287.0 1.0 multiply_reduce_fusion.6
  288.1 1.0 multiply_reduce_fusion.6
  289.2 1.0 multiply_reduce_fusion.6
  290.4 1.0 multiply_reduce_fusion.6
  291.5 1.0 multiply_reduce_fusion.6
  292.6 1.0 multiply_reduce_fusion.6
  293.7 1.0 multiply_reduce_fusion.6
  298.2 1.0 multiply_reduce_fusion.6
  299.3 1.0 multiply_reduce_fusion.6
  300.4 1.0 multiply_reduce_fusion.6
  304.9 1.0 multiply_reduce_fusion.6
  306.0 3.2 all-gather.6.cloned.1.call-done
  309.2 6.1 fusion.20
  315.7 31.9 %reduce-scatter.3.cloned.1.call-done = f32[8,4096]{1,0:T(8,128)} async-done(((f32[64,4096]{1,0:T(8,128)}), f32[8,4096]{1,0:T(8,128)}) %reduce-scatter.3.cloned.1.call-update) | async-done | bytes 131088 | tf_op jit(solution)/shard_map/reduce_scatter | solution.py:101
  347.6 1.1 multiply_reduce_fusion.3
  348.7 1.0 multiply_convert_fusion.2
  350.1 12.0 %all_to_all.30 = bf16[8,4,4096]{2,1,0:T(4,128)(2,1)S(1)} all-to-all(bf16[8,4,4096]{2,1,0:T(4,128)(2,1)S(1)} %all_to_all.19), channel_id=1, replica_groups=mesh['seq'=32,'exp'=8] {'exp'}, dimensions={0} | all-to-all | bytes 524288 | tf_op jit(solution)/shard_map/all_to_all | solution.py:123
  362.2 1.0 stack.5
  363.3 192.7 %all_to_all.31 = bf16[32,32,4096]{2,1,0:T(8,128)(2,1)S(1)} all-to-all(bf16[32,32,4096]{2,1,0:T(8,128)(2,1)S(1)} %stack.5), channel_id=1, replica_groups=mesh['seq'=32,'exp'=8] {'seq'}, dimensions={0} | all-to-all | bytes 16777216 | tf_op jit(solution)/shard_map/all_to_all | solution.py:128
  556.0 3.2 copy-done.2
  559.3 5.2 fusion.5
  564.5 15.5 %convolution_convert_fusion = bf16[1024,4096]{1,0:T(8,128)(2,1)} fusion(bf16[1,448,4096]{2,1,0:T(8,128)(2,1)} %param.38, f32[1024,448]{0,1:T(8,128)} %fusion.5, bf16[1024,4096]{1,0:T(8,128)(2,1)} %bitcast.72, bf16[1,4096,448]{1,2,0:T(8,128)(2,1)} %param.37), kind=kOutput, calls=%fused_computation.9 | convolution fusion | flops 7523139584 | bytes 25952256 | tf_op jit(solution)/shard_map/dot_general | solution.py:134
  580.2 222.7 %reduce-scatter.5.cloned.1.call-done = bf16[32,4096]{1,0:T(8,128)(2,1)} async-done(((bf16[1024,4096]{1,0:T(8,128)(2,1)}), bf16[32,4096]{1,0:T(8,128)(2,1)}) %reduce-scatter.5.cloned.1.call-update) | async-done | bytes 262160 | tf_op jit(solution)/shard_map/reduce_scatter | solution.py:133
  802.9 1.9 reshape.119
  804.8 9.0 %all-to-all-start.2 = ((f32[8,4,4096]{2,1,0:T(4,128)}), f32[8,4,4096]{2,1,0:T(4,128)S(1)}, u32[]{:S(2)}, u32[]{:S(2)}) async-start(f32[8,4,4096]{2,1,0:T(4,128)} %reshape.119), calls=%async_computation.4 | async-start | bytes 1048576 | tf_op jit(solution)/shard_map/all_to_all | solution.py:139
  814.3 9.0 %all-to-all-done.2 = f32[8,4,4096]{2,1,0:T(4,128)S(1)} async-done(((f32[8,4,4096]{2,1,0:T(4,128)}), f32[8,4,4096]{2,1,0:T(4,128)S(1)}, u32[]{:S(2)}, u32[]{:S(2)}) %all-to-all-start.2) | async-done | bytes 524320 | tf_op jit(solution)/shard_map/all_to_all | solution.py:139
  (257 shorter events, 70.3 us)
Async XLA Ops:
  7.2 33.2 %copy-start = (bf16[256,1024]{1,0:T(8,128)(2,1)S(1)}, bf16[256,1024]{1,0:T(8,128)(2,1)}, u32[]{:S(2)}) copy-start(bf16[256,1024]{1,0:T(8,128)(2,1)} %param.28) | copy-start | bytes 1572868
  7.2 119.0 %all-gather.10.cloned.1.call-start = ((), (), s32[]{:S(2)}) async-start(), calls=%async_computation.9 | async-start | bytes 2162688 | tf_op jit(solution)/shard_map/all_gather | solution.py:15
  8.0 4.8 collective-permute-start
  43.2 265.9 %copy-start.6 = (bf16[64,1024]{1,0:T(8,128)(2,1)S(1)}, bf16[64,1024]{1,0:T(8,128)(2,1)}, u32[]{:S(2)}) copy-start(bf16[64,1024]{1,0:T(8,128)(2,1)} %param.23) | copy-start | bytes 393220
  43.2 265.9 %copy-start.8 = (f32[1024]{0:T(1024)S(1)}, f32[1024]{0:T(1024)}, u32[]{:S(2)}) copy-start(f32[1024]{0:T(1024)} %param.31) | copy-start | bytes 12292
  47.6 157.0 %all-gather.8.cloned.1.call-start = ((), (), s32[]{:S(2)}) async-start(), calls=%async_computation.8 | async-start | bytes 2162688 | tf_op jit(solution)/shard_map/all_gather | solution.py:15
  48.3 260.9 %all-gather.6.cloned.1.call-start = ((), (), s32[]{:S(2)}) async-start(), calls=%async_computation.5 | async-start | bytes 8650752 | tf_op jit(solution)/shard_map/all_gather | solution.py:98
  49.0 298.6 %reduce-scatter.3.cloned.1.call-start = ((), (), s32[]{:S(2)}) async-start(), calls=%async_computation.6 | async-start | bytes 1179648 | tf_op jit(solution)/shard_map/reduce_scatter | solution.py:101
  309.2 6.2 copy-start.10
  309.2 38.4 %copy-start.4 = (bf16[8,4096]{1,0:T(8,128)(2,1)S(1)}, bf16[8,4096]{1,0:T(8,128)(2,1)}, u32[]{:S(2)}) copy-start(bf16[8,4096]{1,0:T(8,128)(2,1)} %param.33) | copy-start | bytes 196612
  309.2 39.5 %copy-start.9 = (f32[4096]{0:T(1024)S(1)}, f32[4096]{0:T(1024)}, u32[]{:S(2)}) copy-start(f32[4096]{0:T(1024)} %param.34) | copy-start | bytes 49156
  315.3 487.6 %reduce-scatter.5.cloned.1.call-start = ((), (), s32[]{:S(2)}) async-start(), calls=%async_computation.7 | async-start | bytes 8650752 | tf_op jit(solution)/shard_map/reduce_scatter | solution.py:133
  363.3 196.0 %copy-start.11 = (bf16[1,4096,448]{1,2,0:T(8,128)(2,1)S(1)}, bf16[1,4096,448]{1,2,0:T(8,128)(2,1)}, u32[]{:S(2)}) copy-start(bf16[1,4096,448]{1,2,0:T(8,128)(2,1)} %param.36) | copy-start | bytes 11010052
  556.0 3.2 copy-start.2
  580.0 233.8 %copy-start.7 = (f32[4096,8]{0,1:T(8,128)S(1)}, f32[4096,8]{0,1:T(8,128)}, u32[]{:S(2)}) copy-start(f32[4096,8]{0,1:T(8,128)} %param.35) | copy-start | bytes 393220
  580.0 244.7 %copy-start.3 = (f32[8,4096]{1,0:T(8,128)S(1)}, f32[8,4096]{1,0:T(8,128)}, u32[]{:S(2)}) copy-start(f32[8,4096]{1,0:T(8,128)} %reduce-scatter.3.cloned.1.call-done) | copy-start | bytes 393220
  580.0 245.4 %copy-start.1 = (bf16[256,1024]{1,0:T(8,128)(2,1)S(1)}, bf16[256,1024]{1,0:T(8,128)(2,1)}, u32[]{:S(2)}) copy-start(bf16[256,1024]{1,0:T(8,128)(2,1)} %param.28) | copy-start | bytes 1572868
  804.8 18.5 %all-to-all-start.2 = ((f32[8,4,4096]{2,1,0:T(4,128)}), f32[8,4,4096]{2,1,0:T(4,128)S(1)}, u32[]{:S(2)}, u32[]{:S(2)}) async-start(f32[8,4,4096]{2,1,0:T(4,128)} %reshape.119), calls=%async_computation.4 | async-start | bytes 1048576 | tf_op jit(solution)/shard_map/all_to_all | solution.py:139
  824.7 0.7 copy-start.5
Sparse Core Ops, SparseCore 0:
  47.7 78.4 all-gather.9
  129.4 75.1 all-gather.7
  207.0 102.1 all-gather.5
  315.4 32.1 reduce-scatter.2
  580.1 222.7 reduce-scatter.4
